TPU v7x, 512 devices: a whole 4x4x16 slice. The times are simulated.
512 devices in a mesh: fsdp: 64 (over y, z), layer: 8 (over x, core).
Axes of the slice: x: 4, y: 4, z: 16, core: 2. Of those that a mesh axis runs over, the one named last changes fastest.
Arguments:
- pseudo_gradient: bfloat16 [1024, 16, 4096], P('fsdp', 'layer'), parts along dimension 1, may hold values from -6 to 6
- left_root: bfloat16 [64, 8192, 1024], P('fsdp', 'layer'), parts along dimension 1, may hold values from -1 to 4
- right_root: bfloat16 [64, 1024, 128], P('fsdp', 'layer'), parts along dimension 1, may hold values from -1 to 4
Outputs:
- update: bfloat16 [1024, 16, 4096], P('fsdp', 'layer'), parts along dimension 1
There are 8 independent parts, one for each index of `layer`. A program takes and returns all parts, laid end to end along the dimension named above; each array names one. Nothing has to cross between parts.
All inputs are finite; a program needn't handle non-finite values.
Results may differ from a plain program's by a relative error of at most 0.0049.
Values may be sent and summed in bfloat16 or wider, within the bound.
A program may use at most 64 MiB of HBM per device.

v0:
```python
import jax
import jax.numpy as jnp
from jax import lax
from jax.sharding import PartitionSpec as P

HD = 128


def shards(pseudo_gradient, left_root, right_root):
    local_rows = pseudo_gradient.shape[0]
    pieces = pseudo_gradient.reshape(local_rows, -1, HD)
    product = jnp.einsum(
        "rud,ude->rue",
        pieces,
        lax.all_gather(right_root, "fsdp", axis=0, tiled=True),
        preferred_element_type=jnp.float32,
    )
    scaled = product.astype(jnp.bfloat16)
    product = jnp.dot(
        left_root[0],
        lax.all_to_all(scaled, "fsdp", split_axis=1, concat_axis=0, tiled=True)[:, 0, :],
        preferred_element_type=jnp.float32,
    )
    scaled_back = product.astype(jnp.bfloat16)[:, None, :]
    returned = lax.all_to_all(scaled_back, "fsdp", split_axis=0, concat_axis=1, tiled=True)
    return returned.reshape(pseudo_gradient.shape)


def solution(mesh):
    in_specs = (P("fsdp", "layer", None), P("fsdp", "layer", None), P("fsdp", "layer", None))
    out_specs = P("fsdp", "layer", None)
    return jax.shard_map(shards, mesh=mesh, in_specs=in_specs, out_specs=out_specs, check_vma=False)
```

profile of v0, /device:TPU:6, one launch (start us, length us, event | category | flops | bytes accessed | tf_op | source)
XLA Modules:
  0.0 218.0 jit_solution(11089084479190677917)
XLA Ops:
  6.5 0.0 copy-start
  6.5 0.0 all-gather.2.cloned.1.call-start
  6.5 0.7 all-gather.2.cloned.1.call-update
  7.3 1.2 reshape.8
  8.4 147.3 %all-gather.2.cloned.1.call-done = bf16[64,128,128]{2,1,0:T(8,128)(2,1)} async-done(((bf16[1,128,128]{2,1,0:T(8,128)(2,1)}), bf16[64,128,128]{2,1,0:T(8,128)(2,1)}) %all-gather.2.cloned.1.call-update) | async-done | bytes 2097168 | tf_op jit(solution)/shard_map/all_gather | solution.py:15
  155.7 2.2 %fusion.5 = bf16[16,64,128]{2,0,1:T(8,128)(2,1)S(1)} fusion(bf16[64,128,128]{2,1,0:T(8,128)(2,1)} %all-gather.2.cloned.1.call-done, bf16[16,64,128]{2,1,0:T(8,128)(2,1)S(1)} %reshape.8), kind=kOutput, calls=%fused_computation.4 | convolution fusion | flops 33685504 | bytes 2621440 | tf_op jit(solution)/shard_map/rud,ude->rue/dot_general | solution.py:12
  157.9 26.8 %all_to_all.30 = bf16[16,64,128]{2,0,1:T(8,128)(2,1)S(1)} all-to-all(bf16[16,64,128]{2,0,1:T(8,128)(2,1)S(1)} %fusion.5), channel_id=1, replica_groups=mesh['fsdp'=64,'layer'=8] {'fsdp'}, dimensions={1} | all-to-all | bytes 524288 | tf_op jit(solution)/shard_map/all_to_all | solution.py:21
  184.7 0.0 copy-done
  184.7 0.8 fusion.6
  185.6 0.5 broadcast
  186.1 0.8 reduce
  186.9 0.2 copy.17
  187.1 0.1 reshape.10
  187.1 22.9 %all_to_all.31 = bf16[64,2,1024]{2,1,0:T(2,128)(2,1)S(1)} all-to-all(bf16[64,2,1024]{2,1,0:T(2,128)(2,1)S(1)} %reshape.10), channel_id=1, replica_groups=mesh['fsdp'=64,'layer'=8] {'fsdp'}, dimensions={0} | all-to-all | bytes 524288 | tf_op jit(solution)/shard_map/all_to_all | solution.py:25
  210.1 0.2 reshape.11
  210.4 0.1 copy.13
  210.4 0.8 reshape.9
  (1 shorter events, 0.0 us)
Async XLA Ops:
  6.5 178.2 %copy-start = (bf16[1,1024,1024]{2,1,0:T(8,128)(2,1)S(1)}, bf16[1,1024,1024]{2,1,0:T(8,128)(2,1)}, u32[]{:S(2)}) copy-start(bf16[1,1024,1024]{2,1,0:T(8,128)(2,1)} %param.4) | copy-start | bytes 6291460
  6.5 149.2 %all-gather.2.cloned.1.call-start = ((), (), s32[]{:S(2)}) async-start(), calls=%async_computation.2 | async-start | bytes 2129920 | tf_op jit(solution)/shard_map/all_gather | solution.py:15
Sparse Core Ops, SparseCore 0:
  10.3 145.3 all-gather.1
where the time goes:
time: 218 us
  waiting for transfers between devices  148 us (68%)
  blocking collectives  49.7 us (23%)
  between operations  13.4 us (6%)
  matrix products  3.06 us (1%)
  local copies, waits for them, and re-layouts  3 us (1%)
    all_gather x1, waiting for transfers between devices, shards(): lax.all_gather(right_root, 'fsdp', axis=0, tiled=True)  147 us
    all_to_all x1, blocking collectives, shards(): lax.all_to_all(scaled, 'fsdp', split_axis=1, concat_axis=0, tiled=True)  26.8 us
    all_to_all x1, blocking collectives, shards(): lax.all_to_all(scaled_back, 'fsdp', split_axis=0, concat_axis=1, tiled=True)  22.9 us
  transfers between devices with their start and end apart: 1, of which 1 were waited for; matrix products, arithmetic and copies ran while one was open for 1% of the time, Pallas kernels for 0%

commit v1 on v0

v1 whole, which is shorter than its diff:
```python
import jax
import jax.numpy as jnp
from jax import lax
from jax.sharding import PartitionSpec as P

HD = 128


def shards(pseudo_gradient, left_root, right_root):
    local_rows = pseudo_gradient.shape[0]
    pieces = pseudo_gradient.reshape(local_rows, -1, HD)
    block = lax.all_to_all(pieces, "fsdp", split_axis=1, concat_axis=0, tiled=True)[:, 0, :]
    right = jnp.dot(block, right_root[0], preferred_element_type=jnp.float32).astype(jnp.bfloat16)
    update = jnp.dot(left_root[0], right, preferred_element_type=jnp.float32).astype(jnp.bfloat16)
    returned = lax.all_to_all(update[:, None, :], "fsdp", split_axis=0, concat_axis=1, tiled=True)
    return returned.reshape(pseudo_gradient.shape)


def solution(mesh):
    in_specs = (P("fsdp", "layer", None), P("fsdp", "layer", None), P("fsdp", "layer", None))
    out_specs = P("fsdp", "layer", None)
    return jax.shard_map(shards, mesh=mesh, in_specs=in_specs, out_specs=out_specs, check_vma=False)
```

time: 218 us -> 72.2 us (0.33)
  waiting for transfers between devices: 148 us -> 0 us
  blocking collectives: 49.7 us -> 66 us
  between operations: 13.4 us -> 0.06 us
    all_gather x1 -> x0, waiting for transfers between devices: 147 us -> none  [shards(): lax.all_gather(right_root, 'fsdp', axis=0, tiled=True)]
    all_to_all x2, blocking collectives: 49.7 us -> 66 us  [the longest x1 39.5 us: shards(): lax.all_to_all(pieces, 'fsdp', split_axis=1, concat_axis=0, tiled=True)]
  transfers between devices with their start and end apart: 1 -> 0, of which waited for: 1 -> 0; matrix products, arithmetic and copies ran while one was open for 1% -> 0% of each run, Pallas kernels for 0% -> 0%
where the time goes in v1:
time: 72.2 us; the launch traced here: 71.9 us
  blocking collectives  66 us (91%)
  local copies, waits for them, and re-layouts  3.33 us (5%)
  matrix products  1.75 us (2%)
  other arithmetic  0.78 us (1%)
    all_to_all x1, blocking collectives, shards(): lax.all_to_all(pieces, 'fsdp', split_axis=1, concat_axis=0, tiled=True)  39.5 us
    all_to_all x1, blocking collectives, shards(): lax.all_to_all(update[:, None, :], 'fsdp', split_axis=0, concat_axis=1, t...  26.5 us
    dot_general x1, matrix products, shards(): jnp.dot(left_root[0], right, preferred_element_type=jnp.float32)  1.75 us
    reshape x2, local copies, waits for them, and re-layouts, shards(): pieces = pseudo_gradient.reshape(local_rows, -1, HD)  1.48 us

profile of v1, /device:TPU:6, one launch (start us, length us, event | category | flops | bytes accessed | tf_op | source)
XLA Modules:
  0.0 71.9 jit_solution(5432421921408670235)
XLA Ops:
  0.0 0.0 copy-start
  0.0 1.3 %reshape.8 = bf16[16,64,128]{2,1,0:T(8,128)(2,1)S(1)} reshape(bf16[16,2,4096]{2,1,0:T(2,128)(2,1)} %param.3) | data formatting | bytes 524288 | tf_op jit(solution)/shard_map/reshape | solution.py:11
  1.3 0.2 copy.9
  1.5 39.5 %all_to_all.30 = bf16[16,64,128]{2,0,1:T(8,128)(2,1)S(1)} all-to-all(bf16[16,64,128]{2,0,1:T(8,128)(2,1)S(1)} %copy.9), channel_id=1, replica_groups=mesh['fsdp'=64,'layer'=8] {'fsdp'}, dimensions={1} | all-to-all | bytes 524288 | tf_op jit(solution)/shard_map/all_to_all | solution.py:12
  41.0 0.0 copy-done
  41.0 1.8 %fusion.5 = bf16[1024,1,128]{0,2,1:T(8,128)(2,1)S(1)} fusion(bf16[1,1024,1024]{2,1,0:T(8,128)(2,1)S(1)} %copy-done, bf16[1024,128]{1,0:T(8,128)(2,1)S(1)} %bitcast.29, bf16[1,128,128]{2,1,0:T(8,128)(2,1)} %param.5), kind=kOutput, calls=%fused_computation.4 | convolution fusion | flops 302252032 | bytes 2654208 | tf_op jit(solution)/shard_map/dot_general | solution.py:14
  42.8 0.5 broadcast
  43.3 0.8 %reduce = bf16[1024,128]{0,1:T(8,128)(2,1)S(1)} reduce(bf16[1024,1,128]{0,2,1:T(8,128)(2,1)S(1)} %fusion.5, bf16[]{:T(256)} %broadcast), dimensions={1}, to_apply=%copy.10.reduce_sub_computation | reduce | bytes 524290 | tf_op jit(solution)/shard_map/broadcast_in_dim | solution.py:15
  44.1 0.2 copy.13
  44.2 0.1 reshape.10
  44.3 26.5 %all_to_all.31 = bf16[64,2,1024]{2,1,0:T(2,128)(2,1)S(1)} all-to-all(bf16[64,2,1024]{2,1,0:T(2,128)(2,1)S(1)} %reshape.10), channel_id=1, replica_groups=mesh['fsdp'=64,'layer'=8] {'fsdp'}, dimensions={0} | all-to-all | bytes 524288 | tf_op jit(solution)/shard_map/all_to_all | solution.py:15
  70.8 0.2 reshape.11
  71.1 0.1 copy.11
  71.1 0.8 %reshape.9 = bf16[16,2,4096]{2,1,0:T(2,128)(2,1)} reshape(bf16[16,64,1,128]{3,1,0,2:T(8,128)(2,1)S(1)} %copy.11) | data formatting | bytes 524288 | tf_op jit(solution)/shard_map/reshape | solution.py:16
  (1 shorter events, 0.0 us)
Async XLA Ops:
  0.0 41.0 %copy-start = (bf16[1,1024,1024]{2,1,0:T(8,128)(2,1)S(1)}, bf16[1,1024,1024]{2,1,0:T(8,128)(2,1)}, u32[]{:S(2)}) copy-start(bf16[1,1024,1024]{2,1,0:T(8,128)(2,1)} %param.4) | copy-start | bytes 6291460

commit v2 on v1

v2 whole, which is shorter than its diff:
```python
import jax
import jax.numpy as jnp
from jax import lax
from jax.experimental import pallas as pl
from jax.experimental.pallas import tpu as pltpu
from jax.sharding import PartitionSpec as P

HD = 128
RING = 16
MESH = pl.DeviceIdType.MESH


def partner(me, n, i):
    turn, dy = i // (n // RING), (i + 1) % (n // RING)
    half = (turn + 1) // 2
    dz = RING // 2 + half * (2 * (turn % 2) - 1)
    row, col = me // RING, me % RING
    return (row + dy) % (n // RING) * RING + (col + dz + RING) % RING


def kernel(n, pg_ref, left_ref, right_ref, out_ref, sent, block, left, update, local_sem, send_sem, recv_sem):
    me = lax.axis_index("fsdp")
    rows = pg_ref.shape[0]
    heads = n // pg_ref.shape[1]

    barrier = pltpu.get_barrier_semaphore()

    def greet(i, carry):
        pl.semaphore_signal(barrier, inc=1, device_id={"fsdp": partner(me, n, i)}, device_id_type=MESH)
        return carry

    lax.fori_loop(0, n - 1, greet, 0)
    load = pltpu.make_async_copy(left_ref.at[0], left, local_sem.at[0])
    load.start()
    for b in range(2):
        for h in range(heads):
            sent[b * heads + h] = pg_ref[:, b, h * HD:(h + 1) * HD]
    pl.semaphore_wait(barrier, n - 1)

    def exchange(phase, source, target):
        own = pltpu.make_async_copy(source.at[me], target.at[me], recv_sem.at[phase])
        own.start()

        def send(i, carry):
            to = partner(me, n, i)
            pltpu.make_async_remote_copy(
                src_ref=source.at[to],
                dst_ref=target.at[me],
                send_sem=send_sem.at[phase],
                recv_sem=recv_sem.at[phase],
                device_id={"fsdp": to},
                device_id_type=MESH,
            ).start()
            return carry

        lax.fori_loop(0, n - 1, send, 0)
        pltpu.make_async_copy(source, target, recv_sem.at[phase]).wait()

    exchange(0, sent, block)
    scaled = jnp.dot(block[...].reshape(n * rows, HD), right_ref[0], preferred_element_type=jnp.float32)
    scaled = scaled.astype(jnp.bfloat16)
    load.wait()
    product = jnp.dot(left[...], scaled, preferred_element_type=jnp.float32)
    update[...] = product.astype(jnp.bfloat16).reshape(n, rows, HD)
    exchange(1, update, out_ref)
    for phase in range(2):
        part = sent.at[pl.ds(0, n - 1)]
        pltpu.make_async_copy(part, part, send_sem.at[phase]).wait()


def solution(mesh):
    n = mesh.shape["fsdp"]

    def shards(pseudo_gradient, left_root, right_root):
        rows, blocks, cols = pseudo_gradient.shape
        units = jax.ShapeDtypeStruct((n, rows, HD), jnp.bfloat16)
        vmem = pl.BlockSpec(memory_space=pltpu.VMEM)
        returned = pl.pallas_call(
            lambda *refs: kernel(n, *refs),
            out_shape=units,
            in_specs=[vmem, pl.BlockSpec(memory_space=pl.ANY), vmem],
            out_specs=vmem,
            scratch_shapes=[
                pltpu.VMEM(units.shape, units.dtype),
                pltpu.VMEM(units.shape, units.dtype),
                pltpu.VMEM(left_root.shape[1:], units.dtype),
                pltpu.VMEM(units.shape, units.dtype),
                pltpu.SemaphoreType.DMA((1,)),
                pltpu.SemaphoreType.DMA((2,)),
                pltpu.SemaphoreType.DMA((2,)),
            ],
            compiler_params=pltpu.CompilerParams(
                collective_id=0, has_side_effects=True, vmem_limit_bytes=60 * 1024 * 1024
            ),
        )(pseudo_gradient, left_root, right_root)
        returned = returned.reshape(blocks, cols // HD, rows, HD)
        return returned.transpose(2, 0, 1, 3).reshape(pseudo_gradient.shape)

    specs = P("fsdp", "layer", None)
    return jax.shard_map(shards, mesh=mesh, in_specs=(specs,) * 3, out_specs=specs, check_vma=False)
```

time: 72.2 us -> 50.5 us (0.70)
  blocking collectives: 66 us -> 0 us
  Pallas kernels: 0 us -> 47.9 us
  matrix products: 1.75 us -> 0 us
  local copies, waits for them, and re-layouts: 3.33 us -> 1.79 us
  other arithmetic: 0.78 us -> 0 us
    all_to_all x2 -> x0, blocking collectives: 66 us -> none  [the longest x1 39.5 us: shards(): lax.all_to_all(pieces, 'fsdp', split_axis=1, concat_axis=0, tiled=True)]
    pallas_call x0 -> x1, Pallas kernels: none -> 47.9 us  [shards(): pl.pallas_call(lambda *refs: kernel(n, *refs), out_shape=units, in_specs=...]
    dot_general x1 -> x0, matrix products: 1.75 us -> none  [shards(): jnp.dot(left_root[0], right, preferred_element_type=jnp.float32)]
    reshape x3 -> x1, local copies, waits for them, and re-layouts: 2.25 us -> 0.77 us  [shards(): return returned.transpose(2, 0, 1, 3).reshape(pseudo_gradient.shape)]
    transpose x0 -> x1, local copies, waits for them, and re-layouts: none -> 1.02 us  [shards(): return returned.transpose(2, 0, 1, 3).reshape(pseudo_gradient.shape)]
    broadcast_in_dim x1 -> x0, other arithmetic: 0.78 us -> none  [shards(): update[:, None, :]]
where the time goes in v2:
time: 50.5 us; the launch traced here: 49.7 us
  Pallas kernels  47.9 us (95%)
  local copies, waits for them, and re-layouts  1.79 us (4%)
    pallas_call x1, Pallas kernels, shards(): pl.pallas_call(lambda *refs: kernel(n, *refs), out_shape=units, in_specs=...  47.9 us
    transpose x1, local copies, waits for them, and re-layouts, shards(): return returned.transpose(2, 0, 1, 3).reshape(pseudo_gradient.shape)  1.02 us

profile of v2, /device:TPU:6, one launch (start us, length us, event | category | flops | bytes accessed | tf_op | source)
XLA Modules:
  0.0 49.7 jit_solution(2089457564736684259)
XLA Ops:
  0.0 47.9 %shard_map.37 = bf16[64,16,128]{2,1,0:T(8,128)(2,1)} custom-call(bf16[16,2,4096]{2,1,0:T(2,128)(2,1)} %refs_0_.1, bf16[1,1024,1024]{2,1,0:T(8,128)(2,1)} %refs_1_.1, bf16[1,128,128]{2,1,0:T(8,128)(2,1)} %refs_2_.1), custom_call_target="tpu_custom_call" | custom-call | tf_op jit(solution)/shard_map/pallas_call | solution.py:78
  47.9 1.0 %copy.4 = bf16[16,2,32,128]{3,2,1,0:T(8,128)(2,1)S(1)} copy(bf16[16,2,32,128]{3,0,2,1:T(8,128)(2,1)} %bitcast.5) | data formatting | bytes 524288 | tf_op jit(solution)/shard_map/transpose | solution.py:97
  48.9 0.8 %reshape.7 = bf16[16,2,4096]{2,1,0:T(2,128)(2,1)} reshape(bf16[16,2,32,128]{3,2,1,0:T(8,128)(2,1)S(1)} %copy.4) | data formatting | bytes 524288 | tf_op jit(solution)/shard_map/reshape | solution.py:97

commit v3 on v1

v3 whole, which is shorter than its diff:
```python
import jax
import jax.numpy as jnp
from jax import lax
from jax.experimental import pallas as pl
from jax.experimental.pallas import tpu as pltpu
from jax.sharding import PartitionSpec as P

HD = 128
RING = 16
MESH = pl.DeviceIdType.MESH


def ring_offset(turn):
    half = (turn + 1) // 2
    return (RING // 2 + half * (2 * (turn % 2) - 1) + RING) % RING


def kernel(n, pg_ref, left_ref, right_ref, out_ref, raw, sent, block, left, right, update, back, load_sem, send_sem,
           block_sem, back_sem):
    me = lax.axis_index("fsdp")
    layer = lax.axis_index("layer")
    rows, blocks, _ = pg_ref.shape
    heads = n // blocks
    tall = n // RING
    my_row, my_col = me // RING, me % RING
    mine = (my_row + my_col + layer) % 2

    def device(dy, dz):
        return (my_row + dy) % tall * RING + (my_col + dz) % RING

    def first_partner(i):
        place = i + (1 - mine) * ((i + 1) // (n // 2))
        odd = (mine + place // (n // 2)) % 2
        place = place % (n // 2)
        dz = ring_offset(place // 2)
        return device((odd + dz) % 2 + 2 * (1 - place % 2), dz)

    barrier = pltpu.get_barrier_semaphore()

    def greet(i, carry):
        to = device((i + 1) % tall, ring_offset(i // tall))
        pl.semaphore_signal(barrier, inc=1, device_id={"fsdp": to}, device_id_type=MESH)
        return carry

    lax.fori_loop(0, n - 1, greet, 0)
    loads = [
        pltpu.make_async_copy(pg_ref, raw, load_sem.at[0]),
        pltpu.make_async_copy(right_ref.at[0], right, load_sem.at[1]),
        pltpu.make_async_copy(left_ref.at[0], left, load_sem.at[2]),
    ]
    for load in loads:
        load.start()
    loads[0].wait()
    for h in range(heads):
        pair = raw[:, :, h * HD:(h + 1) * HD].astype(jnp.float32)
        for b in range(blocks):
            sent[b * heads + h] = pair[:, b, :].astype(jnp.bfloat16)
    pl.semaphore_wait(barrier, n - 1)

    def push(source, target, to, phase, sem):
        pltpu.make_async_remote_copy(
            src_ref=source.at[to],
            dst_ref=target.at[me],
            send_sem=send_sem.at[phase],
            recv_sem=sem,
            device_id={"fsdp": to},
            device_id_type=MESH,
        ).start()

    def send_rows(i, carry):
        push(sent, block, first_partner(i), 0, block_sem.at[0])
        return carry

    lax.fori_loop(0, n - 1, send_rows, 0)
    pltpu.make_async_copy(sent.at[me], block.at[me], block_sem.at[0]).start()
    loads[1].wait()
    loads[2].wait()
    pltpu.make_async_copy(sent, block, block_sem.at[0]).wait()
    scaled = jnp.dot(block[...].reshape(n * rows, HD), right[...], preferred_element_type=jnp.float32)
    scaled = scaled.astype(jnp.bfloat16)
    group = RING * rows
    for turn in range(tall):
        dy = (turn + 1) % tall
        row = (my_row + dy) % tall
        part = left[pl.ds(pl.multiple_of(row * group, group), group), :]
        product = jnp.dot(part, scaled, preferred_element_type=jnp.float32)
        update[pl.ds(row * RING, RING)] = product.astype(jnp.bfloat16).reshape(RING, rows, HD)

        def send_back(i, carry):
            push(update, back, device(dy, ring_offset(i)), 1, back_sem.at[mine])
            return carry

        lax.fori_loop(0, RING - (dy == 0), send_back, 0)
    pltpu.make_async_copy(update.at[me], back.at[me], back_sem.at[mine]).start()
    for c in range(2):
        half = back.at[pl.ds(0, n // 2)]
        pltpu.make_async_copy(half, half, back_sem.at[c]).wait()
        for i in range(heads // 2):
            h = 2 * i + (c + layer + i * 2 // RING) % 2
            pair = jnp.stack([back[b * heads + h] for b in range(blocks)], axis=1)
            out_ref[:, :, pl.ds(pl.multiple_of(h * HD, HD), HD)] = pair
    for phase in range(2):
        part = sent.at[pl.ds(0, n - 1)]
        pltpu.make_async_copy(part, part, send_sem.at[phase]).wait()


def solution(mesh):
    n = mesh.shape["fsdp"]

    def shards(pseudo_gradient, left_root, right_root):
        rows = pseudo_gradient.shape[0]
        units = pltpu.VMEM((n, rows, HD), jnp.bfloat16)
        args = [pltpu.with_memory_space_constraint(a, pltpu.HBM) for a in (pseudo_gradient, left_root, right_root)]
        return pl.pallas_call(
            lambda *refs: kernel(n, *refs),
            out_shape=pltpu.VMEM(pseudo_gradient.shape, pseudo_gradient.dtype),
            in_specs=[pl.BlockSpec(memory_space=pltpu.HBM)] * 3,
            out_specs=pl.BlockSpec(memory_space=pltpu.VMEM),
            scratch_shapes=[
                pltpu.VMEM(pseudo_gradient.shape, jnp.bfloat16),
                units,
                units,
                pltpu.VMEM(left_root.shape[1:], jnp.bfloat16),
                pltpu.VMEM(right_root.shape[1:], jnp.bfloat16),
                units,
                units,
                pltpu.SemaphoreType.DMA((3,)),
                pltpu.SemaphoreType.DMA((2,)),
                pltpu.SemaphoreType.DMA((1,)),
                pltpu.SemaphoreType.DMA((2,)),
            ],
            compiler_params=pltpu.CompilerParams(
                collective_id=0, has_side_effects=True, vmem_limit_bytes=32 * 1024 * 1024
            ),
        )(*args)

    specs = P("fsdp", "layer", None)
    return jax.shard_map(shards, mesh=mesh, in_specs=(specs,) * 3, out_specs=specs, check_vma=False)
```

time: 72.2 us -> 44.9 us (0.62)
  blocking collectives: 66 us -> 0 us
  Pallas kernels: 0 us -> 44 us
  local copies, waits for them, and re-layouts: 3.33 us -> 0.71 us
  matrix products: 1.75 us -> 0 us
  other arithmetic: 0.78 us -> 0 us
    all_to_all x2 -> x0, blocking collectives: 66 us -> none  [the longest x1 39.5 us: shards(): lax.all_to_all(pieces, 'fsdp', split_axis=1, concat_axis=0, tiled=True)]
    pallas_call x0 -> x1, Pallas kernels: none -> 44 us  [shards(): pl.pallas_call(lambda *refs: kernel(n, *refs), out_shape=pltpu.VMEM(pseud...]
    reshape x3 -> x0, local copies, waits for them, and re-layouts: 2.25 us -> none  [the longest x2 1.48 us: shards(): pieces = pseudo_gradient.reshape(local_rows, -1, HD)]
    dot_general x1 -> x0, matrix products: 1.75 us -> none  [shards(): jnp.dot(left_root[0], right, preferred_element_type=jnp.float32)]
    broadcast_in_dim x1 -> x0, other arithmetic: 0.78 us -> none  [shards(): update[:, None, :]]
where the time goes in v3:
time: 44.9 us; the launch traced here: 44.8 us
  Pallas kernels  44 us (98%)
  local copies, waits for them, and re-layouts  0.71 us (2%)
    pallas_call x1, Pallas kernels, shards(): pl.pallas_call(lambda *refs: kernel(n, *refs), out_shape=pltpu.VMEM(pseud...  44 us

profile of v3, /device:TPU:6, one launch (start us, length us, event | category | flops | bytes accessed | tf_op | source)
XLA Modules:
  0.0 44.8 jit_solution(10180998399408908692)
XLA Ops:
  0.0 44.0 %shard_map.37 = bf16[16,2,4096]{2,1,0:T(2,128)(2,1)S(1)} custom-call(bf16[16,2,4096]{2,1,0:T(2,128)(2,1)} %refs_0_.1, bf16[1,1024,1024]{2,1,0:T(8,128)(2,1)} %refs_1_.1, bf16[1,128,128]{2,1,0:T(8,128)(2,1)} %refs_2_.1), custom_call_target="tpu_custom_call" | custom-call | tf_op jit(solution)/shard_map/pallas_call | solution.py:114
  44.1 0.7 %copy.5 = bf16[16,2,4096]{2,1,0:T(2,128)(2,1)} copy(bf16[16,2,4096]{2,1,0:T(2,128)(2,1)S(1)} %shard_map.37) | data formatting | bytes 524288

commit v4 on v3

--- a/solution.py
+++ b/solution.py
@@ -78,19 +78,24 @@
     pltpu.make_async_copy(sent, block, block_sem.at[0]).wait()
     scaled = jnp.dot(block[...].reshape(n * rows, HD), right[...], preferred_element_type=jnp.float32)
     scaled = scaled.astype(jnp.bfloat16)
-    group = RING * rows
-    for turn in range(tall):
-        dy = (turn + 1) % tall
-        row = (my_row + dy) % tall
-        part = left[pl.ds(pl.multiple_of(row * group, group), group), :]
-        product = jnp.dot(part, scaled, preferred_element_type=jnp.float32)
-        update[pl.ds(row * RING, RING)] = product.astype(jnp.bfloat16).reshape(RING, rows, HD)
+    quarter = RING // 4
+    for q in range(4):
+        part = left[...].reshape(tall, 4, quarter * rows, n * rows)[:, q].reshape(-1, n * rows)
+        product = jnp.dot(part, scaled, preferred_element_type=jnp.float32).astype(jnp.bfloat16)
+        for y in range(tall):
+            first = y * RING + q * quarter
+            update[first:first + quarter] = product.reshape(tall, quarter, rows, HD)[y]
 
         def send_back(i, carry):
-            push(update, back, device(dy, ring_offset(i)), 1, back_sem.at[mine])
+            to = (my_row + i + 1) % tall * RING + q * quarter + (i // tall + my_col) % quarter
+
+            @pl.when(to != me)
+            def _():
+                push(update, back, to, 1, back_sem.at[mine])
+
             return carry
 
-        lax.fori_loop(0, RING - (dy == 0), send_back, 0)
+        lax.fori_loop(0, quarter * tall, send_back, 0)
     pltpu.make_async_copy(update.at[me], back.at[me], back_sem.at[mine]).start()
     for c in range(2):
         half = back.at[pl.ds(0, n // 2)]

time: 44.9 us -> 42.7 us (0.951)
  Pallas kernels: 44 us -> 41.8 us
    pallas_call x1, Pallas kernels: 44 us -> 41.8 us  [shards(): pl.pallas_call(lambda *refs: kernel(n, *refs), out_shape=pltpu.VMEM(pseud...]
where the time goes in v4:
time: 42.7 us; the launch traced here: 42.5 us
  Pallas kernels  41.8 us (98%)
  local copies, waits for them, and re-layouts  0.71 us (2%)
    pallas_call x1, Pallas kernels, shards(): pl.pallas_call(lambda *refs: kernel(n, *refs), out_shape=pltpu.VMEM(pseud...  41.8 us

profile of v4, /device:TPU:6, one launch (start us, length us, event | category | flops | bytes accessed | tf_op | source)
XLA Modules:
  0.0 42.5 jit_solution(8369165722196153657)
XLA Ops:
  0.0 41.8 %shard_map.37 = bf16[16,2,4096]{2,1,0:T(2,128)(2,1)S(1)} custom-call(bf16[16,2,4096]{2,1,0:T(2,128)(2,1)} %refs_0_.1, bf16[1,1024,1024]{2,1,0:T(8,128)(2,1)} %refs_1_.1, bf16[1,128,128]{2,1,0:T(8,128)(2,1)} %refs_2_.1), custom_call_target="tpu_custom_call" | custom-call | tf_op jit(solution)/shard_map/pallas_call | solution.py:119
  41.8 0.7 %copy.5 = bf16[16,2,4096]{2,1,0:T(2,128)(2,1)} copy(bf16[16,2,4096]{2,1,0:T(2,128)(2,1)S(1)} %shard_map.37) | data formatting | bytes 524288

commit v5 on v4

--- a/solution.py
+++ b/solution.py
@@ -57,18 +57,18 @@
             sent[b * heads + h] = pair[:, b, :].astype(jnp.bfloat16)
     pl.semaphore_wait(barrier, n - 1)
 
-    def push(source, target, to, phase, sem):
+    def push(source, target, to, sent_sem, sem):
         pltpu.make_async_remote_copy(
             src_ref=source.at[to],
             dst_ref=target.at[me],
-            send_sem=send_sem.at[phase],
+            send_sem=sent_sem,
             recv_sem=sem,
             device_id={"fsdp": to},
             device_id_type=MESH,
         ).start()
 
     def send_rows(i, carry):
-        push(sent, block, first_partner(i), 0, block_sem.at[0])
+        push(sent, block, first_partner(i), send_sem.at[0], block_sem.at[0])
         return carry
 
     lax.fori_loop(0, n - 1, send_rows, 0)
@@ -79,23 +79,36 @@
     scaled = jnp.dot(block[...].reshape(n * rows, HD), right[...], preferred_element_type=jnp.float32)
     scaled = scaled.astype(jnp.bfloat16)
     quarter = RING // 4
+    group = quarter * tall
+    core = layer % 2
+
+    def settle(q):
+        here = jnp.where(my_col // quarter == q, 1, 0)
+        for less in range(2):
+            part = sent.at[pl.ds(0, group - less)]
+
+            @pl.when(here == less)
+            def _():
+                pltpu.make_async_copy(part, part, send_sem.at[1 + q]).wait()
+
     for q in range(4):
-        part = left[...].reshape(tall, 4, quarter * rows, n * rows)[:, q].reshape(-1, n * rows)
-        product = jnp.dot(part, scaled, preferred_element_type=jnp.float32).astype(jnp.bfloat16)
+        part = [left[pl.ds((y * RING + q * quarter) * rows, quarter * rows), :] for y in range(tall)]
+        product = jnp.dot(jnp.concatenate(part), scaled, preferred_element_type=jnp.float32).astype(jnp.bfloat16)
         for y in range(tall):
-            first = y * RING + q * quarter
-            update[first:first + quarter] = product.reshape(tall, quarter, rows, HD)[y]
+            update[pl.ds(y * RING + q * quarter, quarter)] = product.reshape(tall, quarter, rows, HD)[y]
+        if q >= 2:
+            pl.when(core == 1)(lambda q=q: settle(q - 2))
 
         def send_back(i, carry):
-            to = (my_row + i + 1) % tall * RING + q * quarter + (i // tall + my_col) % quarter
+            to = i // quarter * RING + q * quarter + (i + my_col) % quarter
 
             @pl.when(to != me)
             def _():
-                push(update, back, to, 1, back_sem.at[mine])
+                push(update, back, to, send_sem.at[1 + q], back_sem.at[mine])
 
             return carry
 
-        lax.fori_loop(0, quarter * tall, send_back, 0)
+        lax.fori_loop(0, group, send_back, 0)
     pltpu.make_async_copy(update.at[me], back.at[me], back_sem.at[mine]).start()
     for c in range(2):
         half = back.at[pl.ds(0, n // 2)]
@@ -104,9 +117,12 @@
             h = 2 * i + (c + layer + i * 2 // RING) % 2
             pair = jnp.stack([back[b * heads + h] for b in range(blocks)], axis=1)
             out_ref[:, :, pl.ds(pl.multiple_of(h * HD, HD), HD)] = pair
-    for phase in range(2):
-        part = sent.at[pl.ds(0, n - 1)]
-        pltpu.make_async_copy(part, part, send_sem.at[phase]).wait()
+    part = sent.at[pl.ds(0, n - 1)]
+    pltpu.make_async_copy(part, part, send_sem.at[0]).wait()
+    for q in range(2):
+        pl.when(core == 0)(lambda q=q: settle(q))
+    for q in range(2, 4):
+        settle(q)
 
 
 def solution(mesh):
@@ -130,7 +146,7 @@
                 units,
                 units,
                 pltpu.SemaphoreType.DMA((3,)),
-                pltpu.SemaphoreType.DMA((2,)),
+                pltpu.SemaphoreType.DMA((5,)),
                 pltpu.SemaphoreType.DMA((1,)),
                 pltpu.SemaphoreType.DMA((2,)),
             ],

time: 42.7 us -> 42.2 us (0.988)
  Pallas kernels: 41.8 us -> 41.3 us
    pallas_call x1, Pallas kernels: 41.8 us -> 41.3 us  [shards(): pl.pallas_call(lambda *refs: kernel(n, *refs), out_shape=pltpu.VMEM(pseud...]
where the time goes in v5:
time: 42.2 us; the launch traced here: 42 us
  Pallas kernels  41.3 us (98%)
  local copies, waits for them, and re-layouts  0.71 us (2%)
    pallas_call x1, Pallas kernels, shards(): pl.pallas_call(lambda *refs: kernel(n, *refs), out_shape=pltpu.VMEM(pseud...  41.3 us

profile of v5, /device:TPU:6, one launch (start us, length us, event | category | flops | bytes accessed | tf_op | source)
XLA Modules:
  0.0 42.0 jit_solution(15923432912460164241)
XLA Ops:
  0.0 41.3 %shard_map.37 = bf16[16,2,4096]{2,1,0:T(2,128)(2,1)S(1)} custom-call(bf16[16,2,4096]{2,1,0:T(2,128)(2,1)} %refs_0_.1, bf16[1,1024,1024]{2,1,0:T(8,128)(2,1)} %refs_1_.1, bf16[1,128,128]{2,1,0:T(8,128)(2,1)} %refs_2_.1), custom_call_target="tpu_custom_call" | custom-call | tf_op jit(solution)/shard_map/pallas_call | solution.py:135
  41.3 0.7 %copy.5 = bf16[16,2,4096]{2,1,0:T(2,128)(2,1)} copy(bf16[16,2,4096]{2,1,0:T(2,128)(2,1)S(1)} %shard_map.37) | data formatting | bytes 524288

commit v6 on v5

--- a/solution.py
+++ b/solution.py
@@ -125,6 +125,18 @@
         settle(q)
 
 
+def store(value_ref, out_ref, sem):
+    rows = out_ref.shape[0] // 2
+    copies = []
+    for c in range(2):
+        part = pl.ds(c * rows, rows)
+        copies.append(pltpu.make_async_copy(value_ref.at[part], out_ref.at[part], sem.at[c]))
+    for copy in copies:
+        copy.start()
+    for copy in copies:
+        copy.wait()
+
+
 def solution(mesh):
     n = mesh.shape["fsdp"]
 
@@ -132,7 +144,7 @@
         rows = pseudo_gradient.shape[0]
         units = pltpu.VMEM((n, rows, HD), jnp.bfloat16)
         args = [pltpu.with_memory_space_constraint(a, pltpu.HBM) for a in (pseudo_gradient, left_root, right_root)]
-        return pl.pallas_call(
+        result = pl.pallas_call(
             lambda *refs: kernel(n, *refs),
             out_shape=pltpu.VMEM(pseudo_gradient.shape, pseudo_gradient.dtype),
             in_specs=[pl.BlockSpec(memory_space=pltpu.HBM)] * 3,
@@ -154,6 +166,13 @@
                 collective_id=0, has_side_effects=True, vmem_limit_bytes=32 * 1024 * 1024
             ),
         )(*args)
+        return pl.pallas_call(
+            store,
+            out_shape=pltpu.HBM(result.shape, result.dtype),
+            in_specs=[pl.BlockSpec(memory_space=pltpu.VMEM)],
+            out_specs=pl.BlockSpec(memory_space=pltpu.HBM),
+            scratch_shapes=[pltpu.SemaphoreType.DMA((2,))],
+        )(pltpu.with_memory_space_constraint(result, pltpu.VMEM))
 
     specs = P("fsdp", "layer", None)
     return jax.shard_map(shards, mesh=mesh, in_specs=(specs,) * 3, out_specs=specs, check_vma=False)

time: 42.2 us -> 42.2 us (level)
  local copies, waits for them, and re-layouts: 0.71 us -> 0 us
  Pallas kernels: 41.3 us -> 42 us
    pallas_call x0 -> x1, Pallas kernels: none -> 0.72 us  [shards(): pl.pallas_call(store, out_shape=pltpu.HBM(result.shape, result.dtype), in...]
    unnamed x1 -> x0, local copies, waits for them, and re-layouts: 0.71 us -> none
where the time goes in v6:
time: 42.2 us; the launch traced here: 42 us
  Pallas kernels  42 us (100%)
    pallas_call x1, Pallas kernels, shards(): pl.pallas_call(lambda *refs: kernel(n, *refs), out_shape=pltpu.VMEM(pseud...  41.3 us

profile of v6, /device:TPU:6, one launch (start us, length us, event | category | flops | bytes accessed | tf_op | source)
XLA Modules:
  0.0 42.0 jit_solution(12221302058856860567)
XLA Ops:
  0.0 41.3 %shard_map.37.value_ref = bf16[16,2,4096]{2,1,0:T(2,128)(2,1)S(1)} custom-call(bf16[16,2,4096]{2,1,0:T(2,128)(2,1)} %refs_0_.1, bf16[1,1024,1024]{2,1,0:T(8,128)(2,1)} %refs_1_.1, bf16[1,128,128]{2,1,0:T(8,128)(2,1)} %refs_2_.1), custom_call_target="tpu_custom_call" | custom-call | tf_op jit(solution)/shard_map/pallas_call | solution.py:147
  41.3 0.7 %shard_map.38 = bf16[16,2,4096]{2,1,0:T(2,128)(2,1)} custom-call(bf16[16,2,4096]{2,1,0:T(2,128)(2,1)S(1)} %shard_map.37.value_ref), custom_call_target="tpu_custom_call" | custom-call | tf_op jit(solution)/shard_map/pallas_call | solution.py:169

commit v7 on v6

--- a/solution.py
+++ b/solution.py
@@ -80,7 +80,7 @@
     scaled = scaled.astype(jnp.bfloat16)
     quarter = RING // 4
     group = quarter * tall
-    core = layer % 2
+    core = layer % 2 * jnp.where(my_col >= quarter, 1, 0)
 
     def settle(q):
         here = jnp.where(my_col // quarter == q, 1, 0)

time: 42.2 us -> 42.2 us (level)
  no operation moved by 1% of the time
where the time goes in v7:
time: 42.2 us; the launch traced here: 42 us
  Pallas kernels  42 us (100%)
    pallas_call x1, Pallas kernels, shards(): pl.pallas_call(lambda *refs: kernel(n, *refs), out_shape=pltpu.VMEM(pseud...  41.3 us

profile of v7, /device:TPU:6, one launch (start us, length us, event | category | flops | bytes accessed | tf_op | source)
XLA Modules:
  0.0 42.0 jit_solution(8552380011846076203)
XLA Ops:
  0.0 41.3 %shard_map.37.value_ref = bf16[16,2,4096]{2,1,0:T(2,128)(2,1)S(1)} custom-call(bf16[16,2,4096]{2,1,0:T(2,128)(2,1)} %refs_0_.1, bf16[1,1024,1024]{2,1,0:T(8,128)(2,1)} %refs_1_.1, bf16[1,128,128]{2,1,0:T(8,128)(2,1)} %refs_2_.1), custom_call_target="tpu_custom_call" | custom-call | tf_op jit(solution)/shard_map/pallas_call | solution.py:147
  41.3 0.7 %shard_map.38 = bf16[16,2,4096]{2,1,0:T(2,128)(2,1)} custom-call(bf16[16,2,4096]{2,1,0:T(2,128)(2,1)S(1)} %shard_map.37.value_ref), custom_call_target="tpu_custom_call" | custom-call | tf_op jit(solution)/shard_map/pallas_call | solution.py:169
